TPU v7x, 32 devices: a whole 2x2x4 slice. The times are simulated.
32 devices in a mesh: strip: 4 (over y, core), tensor: 8 (over z, x).
Axes of the slice: x: 2, y: 2, z: 4, core: 2. Of those that a mesh axis runs over, the one named last changes fastest.
Arguments:
- conv_out: bfloat16 [32, 128, 1536], P('strip', 'tensor'), may hold values from -425 to 425
- out_grad: bfloat16 [32, 128, 1536], P('strip', 'tensor'), may hold values from -6 to 6
- layer_norm_gain: float32 [1536], replicated, may hold values from 0.5 to 2
- layer_norm_bias: float32 [1536], replicated, may hold values from -3 to 3
- w_in: bfloat16 [1536, 6144], P('strip', 'tensor'), may hold values from -0.15625 to 0.15625
- b_in: float32 [6144], P('tensor'), may hold values from -3 to 3
- w_out: bfloat16 [6144, 1536], P('tensor', 'strip'), may hold values from -0.078125 to 0.078125
- layer_scale: float32 [1536], replicated, may hold values from 0.25 to 2
- dw_kernel: float32 [7, 7, 1536], replicated, may hold values from -0.875 to 0.875
Outputs:
- grad_input: bfloat16 [32, 128, 1536], P('strip', 'tensor')
- grad_w_in: float32 [1536, 6144], P('strip', 'tensor')
- grad_w_out: float32 [6144, 1536], P('tensor', 'strip')
All inputs are finite; a program needn't handle non-finite values.
Results may differ from a plain program's by a relative error of at most 0.0063.
Values may be sent and summed in bfloat16 or wider, within the bound.
A program may use at most 128 MiB of HBM per device.

v0:
```python
import math

import jax
import jax.numpy as jnp
from jax import lax
from jax.sharding import PartitionSpec as P

ln_eps = 1e-06
root_half = 0.7071067811865476
density_norm = 0.3989422804014327


def with_halo(block, sides, width):
    for axis, dim in sides:
        count = lax.axis_size(axis)
        forward = [(i, i + 1) for i in range(count - 1)]
        backward = [(target, source) for source, target in forward]
        low = lax.ppermute(
            lax.slice_in_dim(block, block.shape[dim] - width, None, axis=dim), axis, forward
        )
        high = lax.ppermute(lax.slice_in_dim(block, 0, width, axis=dim), axis, backward)
        block = jnp.concatenate([low, block, high], axis=dim)
    return block


def gelu_value(value):
    return 0.5 * value * (1.0 + lax.erf(value * root_half))


def gelu_slope(value):
    return (
        0.5 * (1.0 + lax.erf(value * root_half))
        + value * jnp.exp(-0.5 * value * value) * density_norm
    )


def apply_layer_norm(flattened_rows):
    centre = jnp.mean(flattened_rows, axis=-1, keepdims=True)
    centred = flattened_rows - centre
    spread = jnp.mean(centred * centred, axis=-1, keepdims=True)
    inverse_deviation = lax.rsqrt(spread + ln_eps)
    return (centred * inverse_deviation, inverse_deviation)


def layer_norm_backward(normed_gradient, centred_input, inverse_deviation, layer_norm_gain):
    gain_scaled = normed_gradient * layer_norm_gain
    first_moment = jnp.mean(gain_scaled, axis=-1, keepdims=True)
    second_moment = jnp.mean(gain_scaled * centred_input, axis=-1, keepdims=True)
    return inverse_deviation * (gain_scaled - first_moment - centred_input * second_moment)


def transpose_conv(padded, dw_kernel, image_height, image_breadth):
    taps = dw_kernel.shape[0]
    total = jnp.zeros((image_height, image_breadth, padded.shape[2]), jnp.float32)
    for row_tap in range(taps):
        for col_tap in range(taps):
            start_row = taps - 1 - row_tap
            start_col = taps - 1 - col_tap
            total = (
                total
                + dw_kernel[row_tap, col_tap]
                * padded[
                    start_row : start_row + image_height, start_col : start_col + image_breadth
                ]
            )
    return total


def body(
    conv_out, out_grad, layer_norm_gain, layer_norm_bias, w_in, b_in, w_out, layer_scale, dw_kernel
):
    tile_rows, tile_cols, channel_count = conv_out.shape
    local_count = tile_rows * tile_cols
    flattened_rows = conv_out.astype(jnp.float32).reshape(local_count, channel_count)
    centred_input, inverse_deviation = apply_layer_norm(flattened_rows)
    normed_output = (centred_input * layer_norm_gain + layer_norm_bias).astype(jnp.bfloat16)
    upstream = out_grad.astype(jnp.float32)
    scaled_grad = (upstream.reshape(local_count, channel_count) * layer_scale).astype(jnp.bfloat16)
    w_in_part, w_out_part = (
        lax.all_gather(w_in, "strip", axis=0, tiled=True),
        lax.all_gather(w_out, "strip", axis=1, tiled=True),
    )
    normed_all, scaled_all = (
        lax.all_gather(normed_output, "tensor", axis=0, tiled=True),
        lax.all_gather(scaled_grad, "tensor", axis=0, tiled=True),
    )
    pre_act = jnp.dot(normed_all, w_in_part, preferred_element_type=jnp.float32) + b_in
    hidden_act = gelu_value(pre_act).astype(jnp.bfloat16)
    back_act = lax.dot_general(
        scaled_all, w_out_part, (((1,), (1,)), ((), ())), preferred_element_type=jnp.float32
    )
    back_pre = (back_act * gelu_slope(pre_act)).astype(jnp.bfloat16)
    grad_in = lax.dot_general(
        normed_all, back_pre, (((0,), (0,)), ((), ())), preferred_element_type=jnp.float32
    )
    grad_out = lax.dot_general(
        hidden_act, scaled_all, (((0,), (0,)), ((), ())), preferred_element_type=jnp.float32
    )
    normed_gradient = lax.psum_scatter(
        lax.dot_general(
            back_pre, w_in_part, (((1,), (1,)), ((), ())), preferred_element_type=jnp.float32
        ).astype(jnp.bfloat16),
        "tensor",
        scatter_dimension=0,
        tiled=True,
    ).astype(jnp.float32)
    summed_in, summed_out = (
        lax.psum_scatter(grad_in, "strip", scatter_dimension=0, tiled=True),
        lax.psum_scatter(grad_out, "strip", scatter_dimension=1, tiled=True),
    )
    total_tokens = local_count * lax.axis_size("strip") * lax.axis_size("tensor")
    factor = 1.0 / math.sqrt(total_tokens)
    convolution_gradient = (
        layer_norm_backward(normed_gradient, centred_input, inverse_deviation, layer_norm_gain)
        .astype(jnp.bfloat16)
        .reshape(tile_rows, tile_cols, channel_count)
    )
    margin = dw_kernel.shape[0] // 2
    padded = with_halo(convolution_gradient, (("strip", 0), ("tensor", 1)), margin)
    grad_input = (
        upstream + transpose_conv(padded.astype(jnp.float32), dw_kernel, tile_rows, tile_cols)
    ).astype(jnp.bfloat16)
    return (grad_input, summed_in * factor, summed_out * factor)


def solution(mesh):
    return jax.shard_map(
        body,
        mesh=mesh,
        in_specs=(
            P("strip", "tensor", None),
            P("strip", "tensor", None),
            P(),
            P(),
            P("strip", "tensor"),
            P("tensor"),
            P("tensor", "strip"),
            P(),
            P(),
        ),
        out_specs=(P("strip", "tensor", None), P("strip", "tensor"), P("tensor", "strip")),
        check_vma=False,
    )
```

profile of v0, /device:TPU:0, one launch (start us, length us, event | category | flops | bytes accessed | tf_op | source)
XLA Modules:
  0.0 380.6 jit_solution(10209572125402498076)
XLA Ops:
  7.2 0.0 all-gather.11.cloned.1.call-start
  7.2 0.7 all-gather.11.cloned.1.call-update
  7.9 0.0 all-gather.9.cloned.1.call-start
  8.0 1.1 convert_reduce_fusion
  9.1 0.1 div.16
  9.2 1.2 multiply_reduce_fusion.1
  10.4 0.1 rsqrt.12
  10.5 2.1 add_convert_fusion
  12.6 0.0 all-gather.9.cloned.1.call-update
  12.6 0.0 all-gather.7.cloned.1.call-start
  12.7 0.7 all-gather.7.cloned.1.call-update
  13.4 0.0 all-gather.5.cloned.1.call-start
  13.4 0.8 fusion.60
  14.3 0.0 reduce-scatter.4.cloned.1.call-start
  14.3 22.1 %all-gather.11.cloned.1.call-done = bf16[1536,768]{1,0:T(8,128)(2,1)} async-done(((bf16[384,768]{1,0:T(8,128)(2,1)}), bf16[1536,768]{1,0:T(8,128)(2,1)}) %all-gather.11.cloned.1.call-update) | async-done | bytes 2359312 | tf_op jit(solution)/shard_map/all_gather | solution.py:80
  36.4 63.2 %all-gather.9.cloned.1.call-done = bf16[1024,1536]{1,0:T(8,128)(2,1)} async-done(((bf16[128,1536]{1,0:T(8,128)(2,1)}), bf16[1024,1536]{1,0:T(8,128)(2,1)}) %all-gather.9.cloned.1.call-update) | async-done | bytes 3145744 | tf_op jit(solution)/shard_map/all_gather | solution.py:84
  99.6 5.2 %fusion.64 = f32[1024,768]{1,0:T(8,128)S(1)} fusion(bf16[1024,1536]{1,0:T(8,128)(2,1)} %all-gather.9.cloned.1.call-done, bf16[1536,768]{1,0:T(8,128)(2,1)} %all-gather.11.cloned.1.call-done), kind=kOutput, calls=%fused_computation.184 | convolution fusion | flops 2415919104 | bytes 8650752 | tf_op jit(solution)/shard_map/dot_general | solution.py:87
  104.8 19.0 %all-gather.7.cloned.1.call-done = bf16[768,1536]{1,0:T(8,128)(2,1)} async-done(((bf16[768,384]{1,0:T(8,128)(2,1)}), bf16[768,1536]{1,0:T(8,128)(2,1)}) %all-gather.7.cloned.1.call-update) | async-done | bytes 2359312 | tf_op jit(solution)/shard_map/all_gather | solution.py:81
  123.9 63.1 %all-gather.5.cloned.1.call-done = bf16[1024,1536]{1,0:T(8,128)(2,1)} async-done(((bf16[128,1536]{1,0:T(8,128)(2,1)}), bf16[1024,1536]{1,0:T(8,128)(2,1)}) %all-gather.5.cloned.1.call-update) | async-done | bytes 3145744 | tf_op jit(solution)/shard_map/all_gather | solution.py:85
  187.0 6.0 %fusion.5 = bf16[1024,768]{1,0:T(8,128)(2,1)S(1)} fusion(f32[1024,768]{1,0:T(8,128)S(1)} %fusion.64, bf16[1024,1536]{1,0:T(8,128)(2,1)} %all-gather.5.cloned.1.call-done, bf16[768,1536]{1,0:T(8,128)(2,1)} %all-gather.7.cloned.1.call-done, f32[768]{0:T(1024)S(1)} %copy-done.5), kind=kOutput, calls=%fused_computation.7 | convolution fusion | flops 2424569856 | bytes 10226688 | tf_op jit(solution)/shard_map/dot_general | solution.py:89
  193.0 1.2 copy-done.10
  194.2 4.1 %convolution_convert_fusion = bf16[1024,1536]{1,0:T(8,128)(2,1)} fusion(bf16[1024,768]{1,0:T(8,128)(2,1)S(1)} %fusion.5, bf16[1536,768]{1,0:T(8,128)(2,1)S(1)} %copy-done.9), kind=kOutput, calls=%fused_computation.1 | convolution fusion | flops 2417491968 | bytes 7077888 | tf_op jit(solution)/shard_map/dot_general | solution.py:100
  198.4 0.0 reduce-scatter.6.cloned.1.call-start
  198.4 1.8 copy-done.8
  200.3 5.7 %fusion.65 = f32[1536,768]{1,0:T(8,128)} fusion(bf16[1024,1536]{1,0:T(8,128)(2,1)S(1)} %copy-done.8, bf16[1024,768]{1,0:T(8,128)(2,1)} %copy-done.10), kind=kOutput, calls=%fused_computation.185 | convolution fusion | flops 2415919104 | bytes 9437184 | tf_op jit(solution)/shard_map/dot_general | solution.py:93
  206.0 0.0 reduce-scatter.8.cloned.1.call-start
  206.0 1.8 copy-done.1
  207.9 6.7 %fusion.6 = f32[768,1536]{1,0:T(8,128)} fusion(bf16[1024,1536]{1,0:T(8,128)(2,1)S(1)} %copy-done.1, f32[1024,768]{1,0:T(8,128)} %copy-done.2, f32[768]{0:T(1024)S(1)} %copy-done.5), kind=kOutput, calls=%fused_computation.10 | convolution fusion | flops 2420637696 | bytes 11013120 | tf_op jit(solution)/shard_map/dot_general | solution.py:96
  214.6 56.8 %reduce-scatter.4.cloned.1.call-done = bf16[128,1536]{1,0:T(8,128)(2,1)} async-done(((bf16[1024,1536]{1,0:T(8,128)(2,1)}), bf16[128,1536]{1,0:T(8,128)(2,1)}) %reduce-scatter.4.cloned.1.call-update) | async-done | bytes 393232 | tf_op jit(solution)/shard_map/reduce_scatter | solution.py:99
  271.4 1.3 fusion.61
  272.7 1.3 multiply_convert_fusion.2
  274.0 1.3 collective-permute-start
  275.4 1.5 collective-permute-start.1
  276.8 0.3 slice_reduce_fusion.48
  277.2 0.3 slice_reduce_fusion.47
  277.5 2.9 collective-permute-done.1
  280.3 0.1 pad_maximum_fusion.2
  280.5 3.4 collective-permute-start.2
  283.9 1.3 collective-permute-start.3
  285.2 0.2 slice_reduce_fusion.46
  285.4 1.4 collective-permute-done.2
  286.8 4.4 %collective-permute-done.3 = bf16[14,3,1536]{2,1,0:T(4,128)(2,1)S(1)} collective-permute-done((bf16[14,3,1536]{2,1,0:T(4,128)(2,1)S(1)}, bf16[14,3,1536]{2,1,0:T(4,128)(2,1)S(1)}, u32[]{:S(2)}, u32[]{:S(2)}) %collective-permute-start.3) | collective-permute-done | bytes 129056 | tf_op jit(solution)/shard_map/ppermute | solution.py:21
  291.2 0.4 maximum_convert_fusion
  291.6 6.2 %fusion.11 = bf16[8,16,1536]{2,1,0:T(8,128)(2,1)} fusion(f32[14,22,1536]{2,1,0:T(8,128)S(1)} %maximum_convert_fusion, f32[1536]{0:T(1024)S(1)} %get-tuple-element.52, f32[1536]{0:T(1024)S(1)} %get-tuple-element.53, f32[1536]{0:T(1024)S(1)} %get-tuple-element.6, f32[1536]{0:T(1024)S(1)} %get-tuple-element.7, f32[1536]{0:T(1024)S(1)} %get-tuple-element.8, ...), kind=kLoop, calls=%fused_computation.17 | loop fusion | flops 19660800 | bytes 39622656 | tf_op jit(solution)/shard_map/convert_element_type | solution.py:122
  297.8 23.0 %reduce-scatter.6.cloned.1.call-done = f32[384,768]{1,0:T(8,128)} async-done(((f32[1536,768]{1,0:T(8,128)}), f32[384,768]{1,0:T(8,128)}) %reduce-scatter.6.cloned.1.call-update) | async-done | bytes 1179664 | tf_op jit(solution)/shard_map/reduce_scatter | solution.py:108
  320.8 2.4 broadcast_multiply_fusion.1
  323.2 48.2 %reduce-scatter.8.cloned.1.call-done = f32[768,384]{1,0:T(8,128)} async-done(((f32[768,1536]{1,0:T(8,128)}), f32[768,384]{1,0:T(8,128)}) %reduce-scatter.8.cloned.1.call-update) | async-done | bytes 1179664 | tf_op jit(solution)/shard_map/reduce_scatter | solution.py:109
  371.4 2.4 broadcast_multiply_fusion
  (28 shorter events, 0.1 us)
Async XLA Ops:
  7.2 6.2 %copy-start.3 = (bf16[8,16,1536]{2,1,0:T(8,128)(2,1)S(1)}, bf16[8,16,1536]{2,1,0:T(8,128)(2,1)}, u32[]{:S(2)}) copy-start(bf16[8,16,1536]{2,1,0:T(8,128)(2,1)} %param.10) | copy-start | bytes 1179652
  7.2 6.2 %copy-start.7 = (f32[1536]{0:T(1024)S(1)}, f32[1536]{0:T(1024)}, u32[]{:S(2)}) copy-start(f32[1536]{0:T(1024)} %param.16) | copy-start | bytes 18436
  7.2 29.2 %all-gather.11.cloned.1.call-start = ((), (), s32[]{:S(2)}) async-start(), calls=%async_computation.6 | async-start | bytes 2949120 | tf_op jit(solution)/shard_map/all_gather | solution.py:80
  7.9 91.7 %all-gather.9.cloned.1.call-start = ((), (), s32[]{:S(2)}) async-start(), calls=%async_computation.5 | async-start | bytes 3538944 | tf_op jit(solution)/shard_map/all_gather | solution.py:84
  12.6 111.3 %all-gather.7.cloned.1.call-start = ((), (), s32[]{:S(2)}) async-start(), calls=%async_computation.4 | async-start | bytes 2949120 | tf_op jit(solution)/shard_map/all_gather | solution.py:81
  13.4 173.6 %all-gather.5.cloned.1.call-start = ((), (), s32[]{:S(2)}) async-start(), calls=%async_computation.3 | async-start | bytes 3538944 | tf_op jit(solution)/shard_map/all_gather | solution.py:85
  14.3 172.7 %copy-start.5 = (f32[768]{0:T(1024)S(1)}, f32[768]{0:T(1024)}, u32[]{:S(2)}) copy-start(f32[768]{0:T(1024)} %param.14) | copy-start | bytes 9220
  14.3 257.1 %reduce-scatter.4.cloned.1.call-start = ((), (), s32[]{:S(2)}) async-start(), calls=%async_computation.7 | async-start | bytes 3538944 | tf_op jit(solution)/shard_map/reduce_scatter | solution.py:99
  104.8 88.1 %copy-start.2 = (f32[1024,768]{1,0:T(8,128)}, f32[1024,768]{1,0:T(8,128)S(1)}, u32[]{:S(2)}) copy-start(f32[1024,768]{1,0:T(8,128)S(1)} %fusion.64) | copy-start | bytes 9437188
  187.0 7.2 %copy-start.9 = (bf16[1536,768]{1,0:T(8,128)(2,1)S(1)}, bf16[1536,768]{1,0:T(8,128)(2,1)}, u32[]{:S(2)}) copy-start(bf16[1536,768]{1,0:T(8,128)(2,1)} %all-gather.11.cloned.1.call-done) | copy-start | bytes 7077892
  193.0 1.2 copy-start.10
  198.4 1.9 copy-start.8
  198.4 122.4 %reduce-scatter.6.cloned.1.call-start = ((), (), s32[]{:S(2)}) async-start(), calls=%async_computation.8 | async-start | bytes 5898240 | tf_op jit(solution)/shard_map/reduce_scatter | solution.py:108
  206.0 1.9 copy-start.1
  206.0 165.4 %reduce-scatter.8.cloned.1.call-start = ((), (), s32[]{:S(2)}) async-start(), calls=%async_computation.9 | async-start | bytes 5898240 | tf_op jit(solution)/shard_map/reduce_scatter | solution.py:109
  214.6 56.8 %copy-start = (bf16[8,16,1536]{2,1,0:T(8,128)(2,1)S(1)}, bf16[8,16,1536]{2,1,0:T(8,128)(2,1)}, u32[]{:S(2)}) copy-start(bf16[8,16,1536]{2,1,0:T(8,128)(2,1)} %param.9) | copy-start | bytes 1179652
  214.6 56.8 %copy-start.6 = (f32[1536]{0:T(1024)S(1)}, f32[1536]{0:T(1024)}, u32[]{:S(2)}) copy-start(f32[1536]{0:T(1024)} %param.11) | copy-start | bytes 18436
  214.6 62.2 %copy-start.4 = (f32[7,7,1536]{2,1,0:T(8,128)S(1)}, f32[7,7,1536]{2,1,0:T(8,128)}, u32[]{:S(2)}) copy-start(f32[7,7,1536]{2,1,0:T(8,128)} %param.17) | copy-start | bytes 903172
  274.0 3.4 collective-permute-start
  275.4 5.0 %collective-permute-start.1 = (bf16[3,16,1536]{2,1,0:T(8,128)(2,1)S(1)}, bf16[3,16,1536]{2,1,0:T(8,128)(2,1)S(1)}, u32[]{:S(2)}, u32[]{:S(2)}) collective-permute-start(bf16[3,16,1536]{2,1,0:T(8,128)(2,1)S(1)} %bitcast.28), channel_id=1, source_target_pairs={{8,0},{16,8},{24,16},{9,1},{17,9},{25,17},{10,2},{18,10},{26,18},{... | collective-permute-start | bytes 442376 | tf_op jit(solution)/shard_map/ppermute | solution.py:21
  280.5 6.3 %collective-permute-start.2 = (bf16[14,3,1536]{2,1,0:T(4,128)(2,1)S(1)}, bf16[14,3,1536]{2,1,0:T(4,128)(2,1)S(1)}, u32[]{:S(2)}, u32[]{:S(2)}) collective-permute-start(bf16[14,3,1536]{2,1,0:T(4,128)(2,1)S(1)} %get-tuple-element.54), channel_id=1, source_target_pairs={{0,1},{1,2},{2,3},{3,4},{4,5},{5,6},{6,7},{8,9},{9,10},{10,11},{11... | collective-permute-start | bytes 387080 | tf_op jit(solution)/shard_map/ppermute | solution.py:18
  283.9 7.3 %collective-permute-start.3 = (bf16[14,3,1536]{2,1,0:T(4,128)(2,1)S(1)}, bf16[14,3,1536]{2,1,0:T(4,128)(2,1)S(1)}, u32[]{:S(2)}, u32[]{:S(2)}) collective-permute-start(bf16[14,3,1536]{2,1,0:T(4,128)(2,1)S(1)} %get-tuple-element.55), channel_id=1, source_target_pairs={{1,0},{2,1},{3,2},{4,3},{5,4},{6,5},{7,6},{9,8},{10,9},{11,10},{12... | collective-permute-start | bytes 387080 | tf_op jit(solution)/shard_map/ppermute | solution.py:21
Sparse Core Ops, SparseCore 0:
  9.6 26.7 all-gather.10
  39.1 60.4 all-gather.8
  101.2 22.6 all-gather.6
  126.5 60.4 all-gather.4
  198.5 72.8 reduce-scatter.3
  273.8 47.0 reduce-scatter.5
  323.5 47.8 reduce-scatter.7
where the time goes:
time: 381 us
  waiting for transfers between devices  306 us (80%)
  matrix products  27.8 us (7%)
  other arithmetic  19.4 us (5%)
  between operations  14.3 us (4%)
  starting transfers between devices  7.73 us (2%)
  local copies, waits for them, and re-layouts  5.91 us (2%)
    all_gather x1, waiting for transfers between devices, body(): lax.all_gather(normed_output, 'tensor', axis=0, tiled=True)  63.2 us
    all_gather x1, waiting for transfers between devices, body(): lax.all_gather(scaled_grad, 'tensor', axis=0, tiled=True)  63.1 us
    reduce_scatter x1, waiting for transfers between devices, body(): lax.psum_scatter(lax.dot_general(back_pre, w_in_part, (((1,), (1,)), ((),...  56.8 us
    reduce_scatter x1, waiting for transfers between devices, body(): lax.psum_scatter(grad_out, 'strip', scatter_dimension=1, tiled=True)  48.2 us
    reduce_scatter x1, waiting for transfers between devices, body(): lax.psum_scatter(grad_in, 'strip', scatter_dimension=0, tiled=True)  23 us
    all_gather x1, waiting for transfers between devices, body(): lax.all_gather(w_in, 'strip', axis=0, tiled=True)  22.1 us
    all_gather x1, waiting for transfers between devices, body(): lax.all_gather(w_out, 'strip', axis=1, tiled=True)  19 us
  transfers between devices with their start and end apart: 11, of which 10 were waited for; matrix products, arithmetic and copies ran while one was open for 9% of the time, Pallas kernels for 0%

commit v1 on v0

--- a/solution.py
+++ b/solution.py
@@ -1,13 +1,19 @@
+import functools
 import math
 
 import jax
 import jax.numpy as jnp
 from jax import lax
+from jax.experimental import pallas as pl
+from jax.experimental.pallas import tpu as pltpu
 from jax.sharding import PartitionSpec as P
 
 ln_eps = 1e-06
 root_half = 0.7071067811865476
 density_norm = 0.3989422804014327
+MESH = pl.DeviceIdType.MESH
+F32 = jnp.float32
+BF16 = jnp.bfloat16
 
 
 def with_halo(block, sides, width):
@@ -66,6 +72,369 @@
     return total
 
 
+def nt(a, b):
+    return lax.dot_general(a, b, (((1,), (1,)), ((), ())), preferred_element_type=F32)
+
+
+def tn(a, b):
+    return lax.dot_general(a, b, (((0,), (0,)), ((), ())), preferred_element_type=F32)
+
+
+def block_kernel(
+    factor,
+    conv_ref, grad_ref, gain_ref, bias_ref, win_ref, bin_ref, wout_ref, scale_ref,
+    gconv_ref, gin_ref, gout_ref,
+    tok, win, wout, hid, bp, acc_in, acc_out, xhat, inv,
+    gown, gsend, gxrecv, zsend, zrecv, total,
+    csend_in, csend_out, crecv_in, crecv_out, ysend_in, ysend_out, yrecv_in, yrecv_out,
+    wy_s, wy_r, wc_s, wc_r, az_s, az_r, ax_s, ax_r, gx_s, gx_r, gz_s, gz_r,
+    cs, cr, ys, yr,
+):
+    count, channels = conv_ref.shape
+    shard, wide = win_ref.shape
+    strip = lax.axis_index("strip")
+    tensor = lax.axis_index("tensor")
+    y, core = strip // 2, strip % 2
+    z, x = tensor // 2, tensor % 2
+    up = z // 2
+    zm = z * (1 - up) + (3 - z) * up
+    ypeer = 2 * (1 - y) + core
+    cpeer = 2 * y + 1 - core
+    xpeer = 2 * z + 1 - x
+
+    def unmirror(m):
+        return m * (1 - up) + (3 - m) * up
+
+    def order(i):
+        hi = i // 2
+        return unmirror(hi * i + (1 - hi) * (i + zm - 2 * i * zm))
+
+    def copy(src, dst, s, r, **where):
+        return pltpu.make_async_remote_copy(
+            src_ref=src, dst_ref=dst, send_sem=s, recv_sem=r, device_id=where, device_id_type=MESH
+        )
+
+    def rows(b, xx):
+        return pl.ds(pl.multiple_of((2 * b + xx) * count, count), count)
+
+    barrier = pltpu.get_barrier_semaphore()
+    pl.semaphore_signal(barrier, inc=1, device_id={"strip": ypeer}, device_id_type=MESH)
+    pl.semaphore_signal(barrier, inc=1, device_id={"strip": cpeer}, device_id_type=MESH)
+    pl.semaphore_signal(barrier, inc=1, device_id={"tensor": xpeer}, device_id_type=MESH)
+    for d in range(1, 4):
+        other = 2 * ((z + d) % 4) + x
+        pl.semaphore_signal(barrier, inc=1, device_id={"tensor": other}, device_id_type=MESH)
+
+    def win_rows(s):
+        return win.at[pl.ds(pl.multiple_of(s * shard, shard), shard)]
+
+    def wout_cols(s):
+        return wout.at[:, pl.ds(pl.multiple_of(s * shard, 128), shard)]
+
+    def az_copy(k, h, b, dest):
+        piece = tok.at[h, rows(b, x)]
+        return copy(piece, piece, az_s.at[k, h], az_r.at[b, h], tensor=2 * dest + x)
+
+    def ax_copy(h, b, xx):
+        piece = tok.at[h, rows(b, xx)]
+        return copy(piece, piece, ax_s.at[b, h], ax_r.at[b, h], tensor=xpeer)
+
+    def own_sends(h):
+        az_copy(0, h, z, unmirror(zm + 1)).start()
+
+        @pl.when(zm == 1)
+        def _():
+            az_copy(1, h, z, unmirror(0)).start()
+
+        ax_copy(h, z, x).start()
+
+    wy = [
+        copy(win_ref, win_rows(strip), wy_s.at[0], wy_r.at[0], strip=ypeer),
+        copy(wout_ref, wout_cols(strip), wy_s.at[1], wy_r.at[1], strip=ypeer),
+    ]
+    wc = [
+        copy(win_ref, win_rows(strip), wc_s.at[0], wc_r.at[0], strip=cpeer),
+        copy(wout_ref, wout_cols(strip), wc_s.at[1], wc_r.at[1], strip=cpeer),
+        copy(win_rows(ypeer), win_rows(ypeer), wc_s.at[2], wc_r.at[2], strip=cpeer),
+        copy(wout_cols(ypeer), wout_cols(ypeer), wc_s.at[3], wc_r.at[3], strip=cpeer),
+    ]
+    mine = rows(z, x)
+    tok[0, mine, :] = (grad_ref[...].astype(F32) * scale_ref[...]).astype(BF16)
+    pl.semaphore_wait(barrier, 6)
+    own_sends(0)
+    for c in wy:
+        c.start()
+    for c in wc[:2]:
+        c.start()
+    values, inverse = apply_layer_norm(conv_ref[...].astype(F32))
+    xhat[...] = values
+    inv[...] = inverse
+    tok[1, mine, :] = (values * gain_ref[...] + bias_ref[...]).astype(BF16)
+    own_sends(1)
+    win[pl.ds(pl.multiple_of(strip * shard, shard), shard), :] = win_ref[...]
+    wout[:, pl.ds(pl.multiple_of(strip * shard, 128), shard)] = wout_ref[...]
+    acc_in[...] = jnp.zeros_like(acc_in)
+    acc_out[...] = jnp.zeros_like(acc_out)
+
+    def forward(i):
+        b = order(i)
+        for h in range(2):
+            az_copy(1 + i, h, b, z).wait_recv()
+            ax_copy(h, b, x).start()
+
+            @pl.when(zm == 1)
+            def _():
+                az_copy(1 + i, h, b, unmirror(2 if i == 1 else 0)).start()
+
+    def weights():
+        wy[0].wait_recv()
+        wc[2].start()
+        wy[1].wait_recv()
+        wc[3].start()
+
+    forward(1)
+
+    @pl.when(zm == 1)
+    def _():
+        forward(2)
+
+    weights()
+
+    @pl.when(zm == 0)
+    def _():
+        forward(2)
+
+    for c in wc:
+        c.wait_recv()
+
+    def gx_copy(b):
+        return copy(gsend.at[b], gxrecv.at[b], gx_s.at[b], gx_r.at[b], tensor=xpeer)
+
+    def gz_copy(b):
+        return copy(zsend.at[b], zrecv.at[z], gz_s.at[b], gz_r.at[z], tensor=2 * b + x)
+
+    def reduce(i):
+        b = order(i)
+        gx_copy(b).wait_recv()
+        joined = gown[b] + gxrecv[b].astype(F32)
+
+        @pl.when(b == z)
+        def _():
+            total[...] = joined
+
+        @pl.when(b != z)
+        def _():
+            zsend[b] = joined.astype(BF16)
+            gz_copy(b).start()
+
+    hstep = 256
+    cstep = 256
+
+    @pl.loop(0, 4)
+    def _(i):
+        @pl.when((i == 1) & (zm == 1))
+        def _():
+            forward(3)
+
+        @pl.when((i == 2) & (zm == 0))
+        def _():
+            forward(3)
+
+        b = order(i)
+        for h in range(2):
+            ax_copy(h, b, 1 - x).wait_recv()
+        pair = pl.ds(pl.multiple_of(b * 2 * count, 2 * count), 2 * count)
+
+        @pl.loop(0, wide // hstep)
+        def _(t):
+            cols = pl.ds(pl.multiple_of(t * hstep, hstep), hstep)
+            pre = jnp.dot(tok[1, pair, :], win[:, cols], preferred_element_type=F32)
+            pre = pre + bin_ref[:, cols]
+            back = nt(tok[0, pair, :], wout[cols, :])
+            cdf = 0.5 * (1.0 + lax.erf(pre * root_half))
+            hid[:, cols] = (pre * cdf).astype(BF16)
+            slope = cdf + pre * jnp.exp(-0.5 * pre * pre) * density_norm
+            bp[:, cols] = (back * slope).astype(BF16)
+
+        def normed_grad(xx, put):
+            part = pl.ds(pl.multiple_of(xx * count, count), count)
+
+            @pl.loop(0, channels // cstep)
+            def _(t):
+                chans = pl.ds(pl.multiple_of(t * cstep, cstep), cstep)
+                put(chans, nt(bp[part, :], win[chans, :]))
+
+        def put_send(chans, value):
+            gsend[b, :, chans] = value.astype(BF16)
+
+        def put_own(chans, value):
+            gown[b, :, chans] = value
+
+        normed_grad(1 - x, put_send)
+        gx_copy(b).start()
+        normed_grad(x, put_own)
+
+        @pl.loop(0, channels // cstep)
+        def _(t):
+            chans = pl.ds(pl.multiple_of(t * cstep, cstep), cstep)
+            acc_in[chans, :] += tn(tok[1, pair, chans], bp[...])
+
+        @pl.loop(0, wide // hstep)
+        def _(t):
+            cols = pl.ds(pl.multiple_of(t * hstep, hstep), hstep)
+            acc_out[cols, :] += tn(hid[:, cols], tok[0, pair, :])
+
+        @pl.when(i > 0)
+        def _():
+            reduce(i - 1)
+
+    def in_rows(s):
+        return pl.ds(pl.multiple_of(s * shard, shard), shard)
+
+    def out_cols(s):
+        return pl.ds(pl.multiple_of(s * shard, 128), shard)
+
+    cc = []
+    for k in range(2):
+        yy = (1 - y) * (1 - k) + y * k
+        s = 2 * yy + 1 - core
+        csend_in[k] = acc_in[in_rows(s), :].astype(BF16)
+        c = copy(csend_in.at[k], crecv_in.at[k], cs.at[k, 0], cr.at[k, 0], strip=cpeer)
+        c.start()
+        cc.append(c)
+        csend_out[k] = acc_out[:, out_cols(s)].astype(BF16)
+        c = copy(csend_out.at[k], crecv_out.at[k], cs.at[k, 1], cr.at[k, 1], strip=cpeer)
+        c.start()
+        cc.append(c)
+    reduce(3)
+    cc[0].wait_recv()
+    yc = [
+        copy(ysend_in, yrecv_in, ys.at[0], yr.at[0], strip=ypeer),
+        copy(ysend_out, yrecv_out, ys.at[1], yr.at[1], strip=ypeer),
+    ]
+    ysend_in[...] = (acc_in[in_rows(ypeer), :] + crecv_in[0].astype(F32)).astype(BF16)
+    yc[0].start()
+    cc[1].wait_recv()
+    ysend_out[...] = (acc_out[:, out_cols(ypeer)] + crecv_out[0].astype(F32)).astype(BF16)
+    yc[1].start()
+    cc[2].wait_recv()
+    gin_ref[...] = acc_in[in_rows(strip), :] + crecv_in[1].astype(F32)
+    cc[3].wait_recv()
+    gout_ref[...] = acc_out[:, out_cols(strip)] + crecv_out[1].astype(F32)
+
+    def gz_arrival(b):
+        return copy(zsend.at[b], zrecv.at[b], gz_s.at[b], gz_r.at[b], tensor=2 * b + x)
+
+    for i in range(1, 4):
+        b = order(i)
+        gz_arrival(b).wait_recv()
+        total[...] += zrecv[b].astype(F32)
+    gconv_ref[...] = layer_norm_backward(
+        total[...], xhat[...], inv[...], gain_ref[...]
+    ).astype(BF16)
+
+    yc[0].wait_recv()
+    gin_ref[...] = (gin_ref[...] + yrecv_in[...].astype(F32)) * factor
+    yc[1].wait_recv()
+    gout_ref[...] = (gout_ref[...] + yrecv_out[...].astype(F32)) * factor
+
+    for c in wy + wc + cc + yc:
+        c.wait_send()
+    for h in range(2):
+        for b in range(4):
+            ax_copy(h, b, x).wait_send()
+        az_copy(0, h, z, z).wait_send()
+
+        @pl.when(zm == 1)
+        def _():
+            az_copy(1, h, z, z).wait_send()
+            for i in range(1, 4):
+                az_copy(1 + i, h, order(i), z).wait_send()
+
+    for b in range(4):
+        gx_copy(b).wait_send()
+    for i in range(1, 4):
+        gz_copy(order(i)).wait_send()
+
+
+def fast_body(
+    conv_out, out_grad, layer_norm_gain, layer_norm_bias, w_in, b_in, w_out, layer_scale, dw_kernel
+):
+    tile_rows, tile_cols, channels = conv_out.shape
+    count = tile_rows * tile_cols
+    shard, wide = w_in.shape
+    strips, tensors = lax.axis_size("strip"), lax.axis_size("tensor")
+    tokens = count * tensors
+    factor = 1.0 / math.sqrt(tokens * strips)
+    vmem = pl.BlockSpec(memory_space=pltpu.VMEM)
+    dma = pltpu.SemaphoreType.DMA
+    gconv, gin, gout = pl.pallas_call(
+        functools.partial(block_kernel, factor),
+        out_shape=(
+            jax.ShapeDtypeStruct((count, channels), BF16),
+            jax.ShapeDtypeStruct((shard, wide), F32),
+            jax.ShapeDtypeStruct((wide, shard), F32),
+        ),
+        in_specs=[vmem] * 8,
+        out_specs=(vmem,) * 3,
+        scratch_shapes=[
+            pltpu.VMEM((2, tokens, channels), BF16),
+            pltpu.VMEM((channels, wide), BF16),
+            pltpu.VMEM((wide, channels), BF16),
+            pltpu.VMEM((2 * count, wide), BF16),
+            pltpu.VMEM((2 * count, wide), BF16),
+            pltpu.VMEM((channels, wide), F32),
+            pltpu.VMEM((wide, channels), F32),
+            pltpu.VMEM((count, channels), F32),
+            pltpu.VMEM((count, 1), F32),
+            pltpu.VMEM((4, count, channels), F32),
+            pltpu.VMEM((4, count, channels), BF16),
+            pltpu.VMEM((4, count, channels), BF16),
+            pltpu.VMEM((4, count, channels), BF16),
+            pltpu.VMEM((4, count, channels), BF16),
+            pltpu.VMEM((count, channels), F32),
+            pltpu.VMEM((2, shard, wide), BF16),
+            pltpu.VMEM((2, wide, shard), BF16),
+            pltpu.VMEM((2, shard, wide), BF16),
+            pltpu.VMEM((2, wide, shard), BF16),
+            pltpu.VMEM((shard, wide), BF16),
+            pltpu.VMEM((wide, shard), BF16),
+            pltpu.VMEM((shard, wide), BF16),
+            pltpu.VMEM((wide, shard), BF16),
+            dma((2,)), dma((2,)), dma((4,)), dma((4,)),
+            dma((5, 2)), dma((4, 2)), dma((4, 2)), dma((4, 2)),
+            dma((4,)), dma((4,)), dma((4,)), dma((4,)),
+            dma((2, 2)), dma((2, 2)), dma((2,)), dma((2,)),
+        ],
+        compiler_params=pltpu.CompilerParams(
+            collective_id=0, has_side_effects=True, vmem_limit_bytes=60 * 2**20
+        ),
+        cost_estimate=pl.CostEstimate(
+            flops=10 * tokens * channels * wide,
+            bytes_accessed=12 * shard * wide + 6 * count * channels,
+            transcendentals=2 * tokens * wide,
+        ),
+    )(
+        conv_out.reshape(count, channels),
+        out_grad.reshape(count, channels),
+        layer_norm_gain.reshape(1, channels),
+        layer_norm_bias.reshape(1, channels),
+        w_in,
+        b_in.reshape(1, wide),
+        w_out,
+        layer_scale.reshape(1, channels),
+    )
+    margin = dw_kernel.shape[0] // 2
+    padded = with_halo(
+        gconv.reshape(tile_rows, tile_cols, channels), (("strip", 0), ("tensor", 1)), margin
+    )
+    grad_input = (
+        out_grad.astype(F32)
+        + transpose_conv(padded.astype(F32), dw_kernel, tile_rows, tile_cols)
+    ).astype(BF16)
+    return grad_input, gin, gout
+
+
 def body(
     conv_out, out_grad, layer_norm_gain, layer_norm_bias, w_in, b_in, w_out, layer_scale, dw_kernel
 ):
@@ -124,8 +493,9 @@
 
 
 def solution(mesh):
+    small = mesh.shape["strip"] == 4 and mesh.shape["tensor"] == 8
     return jax.shard_map(
-        body,
+        fast_body if small else body,
         mesh=mesh,
         in_specs=(
             P("strip", "tensor", None),

time: 381 us -> 176 us (0.46)
  waiting for transfers between devices: 306 us -> 8.08 us
  Pallas kernels: 0 us -> 139 us
  matrix products: 27.8 us -> 0 us
  between operations: 14.3 us -> 0.74 us
  other arithmetic: 19.4 us -> 8.86 us
  local copies, waits for them, and re-layouts: 5.91 us -> 10.3 us
    all_gather x4 -> x0, waiting for transfers between devices: 167 us -> none  [the longest x1 63.2 us: body(): lax.all_gather(normed_output, 'tensor', axis=0, tiled=True)]
    pallas_call x0 -> x1, Pallas kernels: none -> 139 us  [fast_body(): pl.pallas_call(functools.partial(block_kernel, factor), out_shape=(jax.Sh...]
    reduce_scatter x3 -> x0, waiting for transfers between devices: 128 us -> none  [the longest x1 56.8 us: body(): lax.psum_scatter(lax.dot_general(back_pre, w_in_part, (((1,), (1,)), ((),...]
    dot_general x5 -> x0, matrix products: 27.8 us -> none  [the longest x1 6.73 us: body(): lax.dot_general(hidden_act, scaled_all, (((0,), (0,)), ((), ())), preferr...]
    reshape x0 -> x4, local copies, waits for them, and re-layouts: none -> 5.15 us  [the longest x1 1.29 us: fast_body(): layer_norm_gain.reshape(1, channels)]
    mul x2 -> x0, other arithmetic: 4.72 us -> none  [body(): return (grad_input, summed_in * factor, summed_out * factor)]
    convert_element_type x5 -> x2, other arithmetic: 10.8 us -> 7.7 us  [the longest x1 7.31 us: fast_body(): grad_input = (out_grad.astype(F32) + transpose_conv(padded.astype(F32), d...]
  transfers between devices with their start and end apart: 11 -> 4, of which waited for: 10 -> 3; matrix products, arithmetic and copies ran while one was open for 9% -> 1% of each run, Pallas kernels for 0% -> 0%
where the time goes in v1:
time: 176 us; the launch traced here: 173 us
  Pallas kernels  139 us (79%)
  local copies, waits for them, and re-layouts  10.3 us (6%)
  other arithmetic  8.86 us (5%)
  waiting for transfers between devices  8.08 us (5%)
  starting transfers between devices  6.33 us (4%)
    pallas_call x1, Pallas kernels, fast_body(): pl.pallas_call(functools.partial(block_kernel, factor), out_shape=(jax.Sh...  139 us
    convert_element_type x1, other arithmetic, fast_body(): grad_input = (out_grad.astype(F32) + transpose_conv(padded.astype(F32), d...  7.31 us
    ppermute x2, waiting for transfers between devices, with_halo(): lax.ppermute(lax.slice_in_dim(block, 0, width, axis=dim), axis, backward)  7.25 us
    ppermute x2, starting transfers between devices, with_halo(): lax.ppermute(lax.slice_in_dim(block, block.shape[dim] - width, None, axis...  3.75 us
  transfers between devices with their start and end apart: 4, of which 3 were waited for; matrix products, arithmetic and copies ran while one was open for 1% of the time, Pallas kernels for 0%

profile of v1, /device:TPU:0, one launch (start us, length us, event | category | flops | bytes accessed | tf_op | source)
XLA Modules:
  0.0 173.2 jit_solution(15554705171923995040)
XLA Ops:
  0.6 1.3 reshape.31.gain_ref
  1.9 1.3 reshape.32.bias_ref
  3.2 1.3 reshape.34.scale_ref
  4.5 1.3 reshape.33.bin_ref
  5.8 0.0 copy-start.3
  5.8 138.9 %shard_map.112 = (bf16[128,1536]{1,0:T(8,128)(2,1)}, f32[384,768]{1,0:T(8,128)}, f32[768,384]{1,0:T(8,128)}) custom-call(bf16[128,1536]{1,0:T(8,128)(2,1)} %bitcast.10, bf16[128,1536]{1,0:T(8,128)(2,1)} %bitcast.7, f32[1,1536]{1,0:T(1,128)} %reshape.31.gain_ref, f32[1,1536]{1,0:T(1,128)} %reshape.32.bias_ref, bf16[384,768]{1,0:T(8,128)(2,1)} %win_ref.1, ...), custom_call_target="tpu_custom_call" | custom-call | flops 12079595520 | bytes 4718592 | tf_op jit(solution)/shard_map/pallas_call | solution.py:371
  144.7 0.0 copy-start
  144.7 1.1 fusion.50
  145.7 1.3 collective-permute-start
  147.0 1.3 collective-permute-start.1
  148.3 0.0 copy-done.3
  148.3 0.3 slice_reduce_fusion.48
  148.7 0.3 slice_reduce_fusion.47
  149.0 0.0 collective-permute-done
  149.0 2.9 %collective-permute-done.1 = bf16[3,16,1536]{2,1,0:T(8,128)(2,1)S(1)} collective-permute-done((bf16[3,16,1536]{2,1,0:T(8,128)(2,1)S(1)}, bf16[3,16,1536]{2,1,0:T(8,128)(2,1)S(1)}, u32[]{:S(2)}, u32[]{:S(2)}) %collective-permute-start.1) | collective-permute-done | bytes 147488 | tf_op jit(solution)/shard_map/ppermute | solution.py:27
  151.8 1.2 pad_maximum_fusion.2
  153.0 2.5 %collective-permute-start.2 = (bf16[14,3,1536]{2,1,0:T(4,128)(2,1)S(1)}, bf16[14,3,1536]{2,1,0:T(4,128)(2,1)S(1)}, u32[]{:S(2)}, u32[]{:S(2)}) collective-permute-start(bf16[14,3,1536]{2,1,0:T(4,128)(2,1)S(1)} %get-tuple-element.58), channel_id=1, source_target_pairs={{0,1},{1,2},{2,3},{3,4},{4,5},{5,6},{6,7},{8,9},{9,10},{10,11},{11... | collective-permute-start | bytes 387080 | tf_op jit(solution)/shard_map/ppermute | solution.py:24
  155.5 1.3 collective-permute-start.3
  156.8 0.8 slice_reduce_fusion.46
  157.5 0.8 collective-permute-done.2
  158.4 4.4 %collective-permute-done.3 = bf16[14,3,1536]{2,1,0:T(4,128)(2,1)S(1)} collective-permute-done((bf16[14,3,1536]{2,1,0:T(4,128)(2,1)S(1)}, bf16[14,3,1536]{2,1,0:T(4,128)(2,1)S(1)}, u32[]{:S(2)}, u32[]{:S(2)}) %collective-permute-start.3) | collective-permute-done | bytes 129056 | tf_op jit(solution)/shard_map/ppermute | solution.py:27
  162.8 0.0 copy-done
  162.8 0.4 maximum_convert_fusion
  163.2 0.0 copy-start.2
  163.2 7.3 %fusion.2 = bf16[8,16,1536]{2,1,0:T(8,128)(2,1)} fusion(f32[14,22,1536]{2,1,0:T(8,128)S(1)} %maximum_convert_fusion, bf16[8,16,1536]{2,1,0:T(8,128)(2,1)} %param.10, f32[1536]{0:T(1024)} %get-tuple-element.56, f32[1536]{0:T(1024)} %get-tuple-element.57, f32[1536]{0:T(1024)S(1)} %get-tuple-element.10, f32[1536]{0:T(1024)S(1)} %get-tuple-element.11, ...), kind=kLoop, calls=%fused_computation.4 | loop fusion | flops 19660800 | bytes 39622656 | tf_op jit(solution)/shard_map/convert_element_type | solution.py:434
  170.5 0.0 copy-done.2
  170.5 0.0 copy-start.1
  170.5 1.0 copy.14
  171.5 0.7 copy-done.1
  172.2 1.0 copy.15
Async XLA Ops:
  5.8 142.6 %copy-start.3 = (f32[7,7,1536]{2,1,0:T(8,128)S(1)}, f32[7,7,1536]{2,1,0:T(8,128)}, u32[]{:S(2)}) copy-start(f32[7,7,1536]{2,1,0:T(8,128)} %param.17) | copy-start | bytes 903172
  144.7 18.1 %copy-start = (bf16[128,1536]{1,0:T(8,128)(2,1)S(1)}, bf16[128,1536]{1,0:T(8,128)(2,1)}, u32[]{:S(2)}) copy-start(bf16[128,1536]{1,0:T(8,128)(2,1)} %get-tuple-element.6) | copy-start | bytes 1179652
  145.7 3.3 %collective-permute-start = (bf16[3,16,1536]{2,1,0:T(8,128)(2,1)S(1)}, bf16[3,16,1536]{2,1,0:T(8,128)(2,1)S(1)}, u32[]{:S(2)}, u32[]{:S(2)}) collective-permute-start(bf16[3,16,1536]{2,1,0:T(8,128)(2,1)S(1)} %bitcast.9), channel_id=1, source_target_pairs={{0,8},{8,16},{16,24},{1,9},{9,17},{17,25},{2,10},{10,18},{18,26},{... | collective-permute-start | bytes 442376 | tf_op jit(solution)/shard_map/ppermute | solution.py:24
  147.0 4.8 %collective-permute-start.1 = (bf16[3,16,1536]{2,1,0:T(8,128)(2,1)S(1)}, bf16[3,16,1536]{2,1,0:T(8,128)(2,1)S(1)}, u32[]{:S(2)}, u32[]{:S(2)}) collective-permute-start(bf16[3,16,1536]{2,1,0:T(8,128)(2,1)S(1)} %bitcast.8), channel_id=1, source_target_pairs={{8,0},{16,8},{24,16},{9,1},{17,9},{25,17},{10,2},{18,10},{26,18},{... | collective-permute-start | bytes 442376 | tf_op jit(solution)/shard_map/ppermute | solution.py:27
  153.0 5.4 %collective-permute-start.2 = (bf16[14,3,1536]{2,1,0:T(4,128)(2,1)S(1)}, bf16[14,3,1536]{2,1,0:T(4,128)(2,1)S(1)}, u32[]{:S(2)}, u32[]{:S(2)}) collective-permute-start(bf16[14,3,1536]{2,1,0:T(4,128)(2,1)S(1)} %get-tuple-element.58), channel_id=1, source_target_pairs={{0,1},{1,2},{2,3},{3,4},{4,5},{5,6},{6,7},{8,9},{9,10},{10,11},{11... | collective-permute-start | bytes 387080 | tf_op jit(solution)/shard_map/ppermute | solution.py:24
  155.5 7.3 %collective-permute-start.3 = (bf16[14,3,1536]{2,1,0:T(4,128)(2,1)S(1)}, bf16[14,3,1536]{2,1,0:T(4,128)(2,1)S(1)}, u32[]{:S(2)}, u32[]{:S(2)}) collective-permute-start(bf16[14,3,1536]{2,1,0:T(4,128)(2,1)S(1)} %get-tuple-element.59), channel_id=1, source_target_pairs={{1,0},{2,1},{3,2},{4,3},{5,4},{6,5},{7,6},{9,8},{10,9},{11,10},{12... | collective-permute-start | bytes 387080 | tf_op jit(solution)/shard_map/ppermute | solution.py:27
  163.2 7.3 %copy-start.2 = (f32[384,768]{1,0:T(8,128)S(1)}, f32[384,768]{1,0:T(8,128)}, u32[]{:S(2)}) copy-start(f32[384,768]{1,0:T(8,128)} %get-tuple-element.66) | copy-start | bytes 3538948
  170.5 1.7 copy-start.1

commit v2 on v1

--- a/solution.py
+++ b/solution.py
@@ -81,14 +81,15 @@
 
 
 def block_kernel(
-    factor,
-    conv_ref, grad_ref, gain_ref, bias_ref, win_ref, bin_ref, wout_ref, scale_ref,
-    gconv_ref, gin_ref, gout_ref,
+    factor, breadth,
+    conv_ref, grad_ref, gain_ref, bias_ref, win_ref, bin_ref, wout_ref, scale_ref, dw_ref,
+    ginput_ref, gin_ref, gout_ref,
     tok, win, wout, hid, bp, acc_in, acc_out, xhat, inv,
     gown, gsend, gxrecv, zsend, zrecv, total,
     csend_in, csend_out, crecv_in, crecv_out, ysend_in, ysend_out, yrecv_in, yrecv_out,
     wy_s, wy_r, wc_s, wc_r, az_s, az_r, ax_s, ax_r, gx_s, gx_r, gz_s, gz_r,
-    cs, cr, ys, yr,
+    vec, bvec, gcb, staged, stage_out, halo_rows, halo_cols, halo_corner, halo_wide, padded,
+    cs, cr, ys, yr, hs, hr, ez_s, ez_r,
 ):
     count, channels = conv_ref.shape
     shard, wide = win_ref.shape
@@ -124,6 +125,26 @@
     for d in range(1, 4):
         other = 2 * ((z + d) % 4) + x
         pl.semaphore_signal(barrier, inc=1, device_id={"tensor": other}, device_id_type=MESH)
+    sides = [(a, b) for a in (-1, 0, 1) for b in (-1, 0, 1) if (a, b) != (0, 0)]
+
+    def inside(a, b):
+        good = None
+        for step, here, size in ((a, strip, 4), (b, tensor, 8)):
+            if step:
+                one = here > 0 if step < 0 else here < size - 1
+                good = one if good is None else good & one
+        return good
+
+    for a, b in sides:
+
+        @pl.when(inside(a, b))
+        def _():
+            pl.semaphore_signal(
+                barrier,
+                inc=1,
+                device_id={"strip": strip + a, "tensor": tensor + b},
+                device_id_type=MESH,
+            )
 
     def win_rows(s):
         return win.at[pl.ds(pl.multiple_of(s * shard, shard), shard)]
@@ -159,8 +180,14 @@
         copy(wout_cols(ypeer), wout_cols(ypeer), wc_s.at[3], wc_r.at[3], strip=cpeer),
     ]
     mine = rows(z, x)
-    tok[0, mine, :] = (grad_ref[...].astype(F32) * scale_ref[...]).astype(BF16)
-    pl.semaphore_wait(barrier, 6)
+    vec[0:1, :] = gain_ref[...].reshape(1, channels)
+    vec[1:2, :] = bias_ref[...].reshape(1, channels)
+    vec[2:3, :] = scale_ref[...].reshape(1, channels)
+    bvec[...] = bin_ref[...].reshape(1, wide)
+    tok[0, mine, :] = (grad_ref[...].astype(F32) * vec[2:3, :]).astype(BF16)
+    above = (strip > 0).astype(jnp.int32) + (strip < 3).astype(jnp.int32)
+    beside = (tensor > 0).astype(jnp.int32) + (tensor < 7).astype(jnp.int32)
+    pl.semaphore_wait(barrier, 6 + above + beside + above * beside)
     own_sends(0)
     for c in wy:
         c.start()
@@ -169,18 +196,25 @@
     values, inverse = apply_layer_norm(conv_ref[...].astype(F32))
     xhat[...] = values
     inv[...] = inverse
-    tok[1, mine, :] = (values * gain_ref[...] + bias_ref[...]).astype(BF16)
+    tok[1, mine, :] = (values * vec[0:1, :] + vec[1:2, :]).astype(BF16)
     own_sends(1)
     win[pl.ds(pl.multiple_of(strip * shard, shard), shard), :] = win_ref[...]
     wout[:, pl.ds(pl.multiple_of(strip * shard, 128), shard)] = wout_ref[...]
     acc_in[...] = jnp.zeros_like(acc_in)
     acc_out[...] = jnp.zeros_like(acc_out)
+    padded[...] = jnp.zeros_like(padded)
 
     def forward(i):
         b = order(i)
         for h in range(2):
             az_copy(1 + i, h, b, z).wait_recv()
-            ax_copy(h, b, x).start()
+            if h == 0 or i == 2:
+                ax_copy(h, b, x).start()
+            elif i == 1:
+
+                @pl.when(zm == 0)
+                def _():
+                    ax_copy(h, b, x).start()
 
             @pl.when(zm == 1)
             def _():
@@ -192,13 +226,29 @@
         wy[1].wait_recv()
         wc[3].start()
 
+    near, far = unmirror(0), unmirror(3)
+
+    def ez_copy(b, dest):
+        piece = tok.at[1, rows(b, 1 - x)]
+        return copy(piece, piece, ez_s.at[b], ez_r.at[b], tensor=2 * dest + x)
+
     forward(1)
 
     @pl.when(zm == 1)
     def _():
         forward(2)
 
+    @pl.when(zm == 0)
+    def _():
+        ax_copy(1, z, 1 - x).wait_recv()
+        ez_copy(near, unmirror(1)).start()
+
     weights()
+
+    @pl.when(zm == 1)
+    def _():
+        ez_copy(near, z).wait_recv()
+        ez_copy(near, unmirror(2)).start()
 
     @pl.when(zm == 0)
     def _():
@@ -207,59 +257,95 @@
     for c in wc:
         c.wait_recv()
 
-    def gx_copy(b):
-        return copy(gsend.at[b], gxrecv.at[b], gx_s.at[b], gx_r.at[b], tensor=xpeer)
-
-    def gz_copy(b):
-        return copy(zsend.at[b], zrecv.at[z], gz_s.at[b], gz_r.at[z], tensor=2 * b + x)
+    half = channels // 2
+
+    def part_of(c):
+        return pl.ds(c * half, half)
+
+    def gx_copy(b, c):
+        src, dst = gsend.at[b, :, part_of(c)], gxrecv.at[b, :, part_of(c)]
+        return copy(src, dst, gx_s.at[b, c], gx_r.at[b, c], tensor=xpeer)
+
+    def gz_copy(b, c):
+        src, dst = zsend.at[b, :, part_of(c)], zrecv.at[z, :, part_of(c)]
+        return copy(src, dst, gz_s.at[b, c], gz_r.at[z, c], tensor=2 * b + x)
+
+    def gz_arrival(b, c):
+        dst = zrecv.at[b, :, part_of(c)]
+        return copy(dst, dst, gz_s.at[b, c], gz_r.at[b, c], tensor=2 * b + x)
 
     def reduce(i):
         b = order(i)
-        gx_copy(b).wait_recv()
-        joined = gown[b] + gxrecv[b].astype(F32)
-
-        @pl.when(b == z)
-        def _():
-            total[...] = joined
-
-        @pl.when(b != z)
-        def _():
-            zsend[b] = joined.astype(BF16)
-            gz_copy(b).start()
+        for c in range(2):
+            part = part_of(c)
+            gx_copy(b, c).wait_recv()
+            joined = gown[b, :, part] + gxrecv[b, :, part].astype(F32)
+
+            @pl.when(b == z)
+            def _():
+                total[:, part] = joined
+
+            @pl.when(b != z)
+            def _():
+                zsend[b, :, part] = joined.astype(BF16)
+                gz_copy(b, c).start()
 
     hstep = 256
     cstep = 256
 
+    def in_rows(s):
+        return pl.ds(pl.multiple_of(s * shard, shard), shard)
+
+    def out_cols(s):
+        return pl.ds(pl.multiple_of(s * shard, 128), shard)
+
+    def other_core(k):
+        return 2 * ((1 - y) * (1 - k) + y * k) + 1 - core
+
+    def core_copy(k, w):
+        send, recv = ((csend_in, crecv_in), (csend_out, crecv_out))[w]
+        return copy(send.at[k], recv.at[k], cs.at[k, w], cr.at[k, w], strip=cpeer)
+
     @pl.loop(0, 4)
     def _(i):
-        @pl.when((i == 1) & (zm == 1))
-        def _():
-            forward(3)
-
-        @pl.when((i == 2) & (zm == 0))
-        def _():
-            forward(3)
-
         b = order(i)
-        for h in range(2):
-            ax_copy(h, b, 1 - x).wait_recv()
+        ax_copy(0, b, 1 - x).wait_recv()
+
+        @pl.when((i == 2) | (i == 1 - zm))
+        def _():
+            ax_copy(1, b, 1 - x).wait_recv()
+
+        @pl.when((i == 3) & (zm == 0))
+        def _():
+            ez_copy(far, z).wait_recv()
+
         pair = pl.ds(pl.multiple_of(b * 2 * count, 2 * count), 2 * count)
 
         @pl.loop(0, wide // hstep)
         def _(t):
             cols = pl.ds(pl.multiple_of(t * hstep, hstep), hstep)
             pre = jnp.dot(tok[1, pair, :], win[:, cols], preferred_element_type=F32)
-            pre = pre + bin_ref[:, cols]
+            pre = pre + bvec[:, cols]
             back = nt(tok[0, pair, :], wout[cols, :])
             cdf = 0.5 * (1.0 + lax.erf(pre * root_half))
             hid[:, cols] = (pre * cdf).astype(BF16)
             slope = cdf + pre * jnp.exp(-0.5 * pre * pre) * density_norm
             bp[:, cols] = (back * slope).astype(BF16)
 
-        def normed_grad(xx, put):
+        @pl.when(i == 1 - zm)
+        def _():
+            forward(3)
+
+        @pl.when((i == 1) & (zm == 1))
+        def _():
+            ez_copy(far, z).wait_recv()
+            ez_copy(far, near).start()
+
+        def normed_grad(xx, c, put):
             part = pl.ds(pl.multiple_of(xx * count, count), count)
-
-            @pl.loop(0, channels // cstep)
+            steps = half // cstep
+
+            @pl.loop(c * steps, (c + 1) * steps)
             def _(t):
                 chans = pl.ds(pl.multiple_of(t * cstep, cstep), cstep)
                 put(chans, nt(bp[part, :], win[chans, :]))
@@ -270,43 +356,45 @@
         def put_own(chans, value):
             gown[b, :, chans] = value
 
-        normed_grad(1 - x, put_send)
-        gx_copy(b).start()
-        normed_grad(x, put_own)
+        for c in range(2):
+            normed_grad(1 - x, c, put_send)
+
+            @pl.when(i > 0)
+            def _():
+                gx_copy(b, c).start()
+
+        @pl.when(i == 3)
+        def _():
+            for c in range(2):
+                gx_copy(z, c).start()
 
         @pl.loop(0, channels // cstep)
         def _(t):
             chans = pl.ds(pl.multiple_of(t * cstep, cstep), cstep)
             acc_in[chans, :] += tn(tok[1, pair, chans], bp[...])
 
+        @pl.when(i == 3)
+        def _():
+            for k in range(2):
+                csend_in[k] = acc_in[in_rows(other_core(k)), :].astype(BF16)
+                core_copy(k, 0).start()
+
+        for c in range(2):
+            normed_grad(x, c, put_own)
+
+        @pl.when(i > 1)
+        def _():
+            reduce(i - 1)
+
         @pl.loop(0, wide // hstep)
         def _(t):
             cols = pl.ds(pl.multiple_of(t * hstep, hstep), hstep)
             acc_out[cols, :] += tn(hid[:, cols], tok[0, pair, :])
 
-        @pl.when(i > 0)
-        def _():
-            reduce(i - 1)
-
-    def in_rows(s):
-        return pl.ds(pl.multiple_of(s * shard, shard), shard)
-
-    def out_cols(s):
-        return pl.ds(pl.multiple_of(s * shard, 128), shard)
-
-    cc = []
     for k in range(2):
-        yy = (1 - y) * (1 - k) + y * k
-        s = 2 * yy + 1 - core
-        csend_in[k] = acc_in[in_rows(s), :].astype(BF16)
-        c = copy(csend_in.at[k], crecv_in.at[k], cs.at[k, 0], cr.at[k, 0], strip=cpeer)
-        c.start()
-        cc.append(c)
-        csend_out[k] = acc_out[:, out_cols(s)].astype(BF16)
-        c = copy(csend_out.at[k], crecv_out.at[k], cs.at[k, 1], cr.at[k, 1], strip=cpeer)
-        c.start()
-        cc.append(c)
-    reduce(3)
+        csend_out[k] = acc_out[:, out_cols(other_core(k))].astype(BF16)
+        core_copy(k, 1).start()
+    cc = [core_copy(k, w) for k in range(2) for w in range(2)]
     cc[0].wait_recv()
     yc = [
         copy(ysend_in, yrecv_in, ys.at[0], yr.at[0], strip=ypeer),
@@ -317,21 +405,95 @@
     cc[1].wait_recv()
     ysend_out[...] = (acc_out[:, out_cols(ypeer)] + crecv_out[0].astype(F32)).astype(BF16)
     yc[1].start()
+    reduce(3)
     cc[2].wait_recv()
     gin_ref[...] = acc_in[in_rows(strip), :] + crecv_in[1].astype(F32)
     cc[3].wait_recv()
     gout_ref[...] = acc_out[:, out_cols(strip)] + crecv_out[1].astype(F32)
 
-    def gz_arrival(b):
-        return copy(zsend.at[b], zrecv.at[b], gz_s.at[b], gz_r.at[b], tensor=2 * b + x)
-
+    reduce(0)
     for i in range(1, 4):
         b = order(i)
-        gz_arrival(b).wait_recv()
+        for c in range(2):
+            gz_arrival(b, c).wait_recv()
         total[...] += zrecv[b].astype(F32)
-    gconv_ref[...] = layer_norm_backward(
-        total[...], xhat[...], inv[...], gain_ref[...]
-    ).astype(BF16)
+    rounded = layer_norm_backward(total[...], xhat[...], inv[...], vec[0:1, :]).astype(BF16)
+    gcb[...] = rounded
+    total[...] = rounded.astype(F32)
+
+    edge = halo_rows.shape[1]
+    quarter = halo_corner.shape[1]
+
+    def side_copy(k, a, b):
+        j = sides.index((-a, -b))
+        if b == 0:
+            src = gcb.at[pl.ds(0 if a < 0 else count - edge, edge)]
+            dst = halo_rows.at[0 if -a < 0 else 1]
+        elif a == 0:
+            src = stage_out.at[0 if b < 0 else 1]
+            dst = halo_cols.at[0 if -b < 0 else 1]
+        else:
+            src = stage_out.at[0 if b < 0 else 1, pl.ds(0 if a < 0 else quarter, quarter)]
+            dst = halo_corner.at[(0 if -a < 0 else 2) + (0 if -b < 0 else 1)]
+        return copy(src, dst, hs.at[k], hr.at[j], strip=strip + a, tensor=tensor + b)
+
+    def side_arrival(k, a, b):
+        if b == 0:
+            dst = halo_rows.at[0 if a < 0 else 1]
+        elif a == 0:
+            dst = halo_cols.at[0 if b < 0 else 1]
+        else:
+            dst = halo_corner.at[(0 if a < 0 else 2) + (0 if b < 0 else 1)]
+        return copy(dst, dst, hs.at[k], hr.at[k], strip=strip + a, tensor=tensor + b)
+
+    def each_side(act, kinds):
+        for k, (a, b) in enumerate(sides):
+            if (b == 0) == kinds or kinds is None:
+
+                @pl.when(inside(a, b))
+                def _():
+                    act(k, a, b)
+
+    each_side(lambda k, a, b: side_copy(k, a, b).start(), True)
+    height = count // breadth
+    for r in range(height):
+        staged[0, 4 * r : 4 * r + 4, :] = total[breadth * r : breadth * r + 4, :]
+        staged[1, 4 * r : 4 * r + 4, :] = total[breadth * (r + 1) - 4 : breadth * (r + 1), :]
+    stage_out[...] = staged[...].astype(BF16)
+    each_side(lambda k, a, b: side_copy(k, a, b).start(), False)
+    for r in range(height):
+        padded[3 + r, 8 : 8 + breadth, :] = total[breadth * r : breadth * (r + 1), :]
+
+    def take(k, a, b):
+        side_arrival(k, a, b).wait_recv()
+        base = 0 if a < 0 else 3 + height
+        left = 4 if b < 0 else 8 + breadth
+        if b == 0:
+            halo_wide[0:edge, :] = halo_rows[0 if a < 0 else 1].astype(F32)
+            for n in range(3):
+                padded[base + n, 8 : 8 + breadth, :] = halo_wide[breadth * n : breadth * (n + 1), :]
+        elif a == 0:
+            halo_wide[0 : 4 * height, :] = halo_cols[0 if b < 0 else 1].astype(F32)
+            for r in range(height):
+                padded[3 + r, left : left + 4, :] = halo_wide[4 * r : 4 * r + 4, :]
+        else:
+            corner = halo_corner[(0 if a < 0 else 2) + (0 if b < 0 else 1)]
+            halo_wide[0:quarter, :] = corner.astype(F32)
+            for n in range(3):
+                r = n + 1 if a < 0 else n
+                padded[base + n, left : left + 4, :] = halo_wide[4 * r : 4 * r + 4, :]
+
+    each_side(take, None)
+
+    @pl.loop(0, channels // 128)
+    def _(t):
+        chans = pl.ds(pl.multiple_of(t * 128, 128), 128)
+        result = grad_ref[:, chans].astype(F32).reshape(height, breadth, 128)
+        for q in range(7):
+            moved = padded[:, 11 - q : 11 - q + breadth, chans]
+            for p in range(7):
+                result = result + dw_ref[p, q : q + 1, chans] * moved[6 - p : 6 - p + height]
+        ginput_ref[:, chans] = result.reshape(count, 128).astype(BF16)
 
     yc[0].wait_recv()
     gin_ref[...] = (gin_ref[...] + yrecv_in[...].astype(F32)) * factor
@@ -340,21 +502,32 @@
 
     for c in wy + wc + cc + yc:
         c.wait_send()
+    each_side(lambda k, a, b: side_copy(k, a, b).wait_send(), None)
+    for i in range(4):
+        ax_copy(0, order(i), x).wait_send()
+    ax_copy(1, z, x).wait_send()
+    ax_copy(1, order(2), x).wait_send()
+    ez_copy(near, z).wait_send()
     for h in range(2):
-        for b in range(4):
-            ax_copy(h, b, x).wait_send()
         az_copy(0, h, z, z).wait_send()
 
-        @pl.when(zm == 1)
-        def _():
+    @pl.when(zm == 0)
+    def _():
+        ax_copy(1, order(1), x).wait_send()
+
+    @pl.when(zm == 1)
+    def _():
+        ez_copy(far, z).wait_send()
+        for h in range(2):
             az_copy(1, h, z, z).wait_send()
             for i in range(1, 4):
                 az_copy(1 + i, h, order(i), z).wait_send()
 
-    for b in range(4):
-        gx_copy(b).wait_send()
-    for i in range(1, 4):
-        gz_copy(order(i)).wait_send()
+    for c in range(2):
+        for b in range(4):
+            gx_copy(b, c).wait_send()
+        for i in range(1, 4):
+            gz_copy(order(i), c).wait_send()
 
 
 def fast_body(
@@ -368,14 +541,14 @@
     factor = 1.0 / math.sqrt(tokens * strips)
     vmem = pl.BlockSpec(memory_space=pltpu.VMEM)
     dma = pltpu.SemaphoreType.DMA
-    gconv, gin, gout = pl.pallas_call(
-        functools.partial(block_kernel, factor),
+    grad_input, gin, gout = pl.pallas_call(
+        functools.partial(block_kernel, factor, tile_cols),
         out_shape=(
             jax.ShapeDtypeStruct((count, channels), BF16),
             jax.ShapeDtypeStruct((shard, wide), F32),
             jax.ShapeDtypeStruct((wide, shard), F32),
         ),
-        in_specs=[vmem] * 8,
+        in_specs=[vmem] * 9,
         out_specs=(vmem,) * 3,
         scratch_shapes=[
             pltpu.VMEM((2, tokens, channels), BF16),
@@ -403,8 +576,19 @@
             pltpu.VMEM((wide, shard), BF16),
             dma((2,)), dma((2,)), dma((4,)), dma((4,)),
             dma((5, 2)), dma((4, 2)), dma((4, 2)), dma((4, 2)),
-            dma((4,)), dma((4,)), dma((4,)), dma((4,)),
-            dma((2, 2)), dma((2, 2)), dma((2,)), dma((2,)),
+            dma((4, 2)), dma((4, 2)), dma((4, 2)), dma((4, 2)),
+            pltpu.VMEM((8, channels), F32),
+            pltpu.VMEM((1, wide), F32),
+            pltpu.VMEM((count, channels), BF16),
+            pltpu.VMEM((2, 4 * tile_rows, channels), F32),
+            pltpu.VMEM((2, 4 * tile_rows, channels), BF16),
+            pltpu.VMEM((2, 3 * tile_cols, channels), BF16),
+            pltpu.VMEM((2, 4 * tile_rows, channels), BF16),
+            pltpu.VMEM((4, 2 * tile_rows, channels), BF16),
+            pltpu.VMEM((3 * tile_cols, channels), F32),
+            pltpu.VMEM((tile_rows + 6, tile_cols + 16, channels), F32),
+            dma((2, 2)), dma((2, 2)), dma((2,)), dma((2,)), dma((8,)), dma((8,)),
+            dma((4,)), dma((4,)),
         ],
         compiler_params=pltpu.CompilerParams(
             collective_id=0, has_side_effects=True, vmem_limit_bytes=60 * 2**20
@@ -417,22 +601,15 @@
     )(
         conv_out.reshape(count, channels),
         out_grad.reshape(count, channels),
-        layer_norm_gain.reshape(1, channels),
-        layer_norm_bias.reshape(1, channels),
+        layer_norm_gain,
+        layer_norm_bias,
         w_in,
-        b_in.reshape(1, wide),
+        b_in,
         w_out,
-        layer_scale.reshape(1, channels),
-    )
-    margin = dw_kernel.shape[0] // 2
-    padded = with_halo(
-        gconv.reshape(tile_rows, tile_cols, channels), (("strip", 0), ("tensor", 1)), margin
-    )
-    grad_input = (
-        out_grad.astype(F32)
-        + transpose_conv(padded.astype(F32), dw_kernel, tile_rows, tile_cols)
-    ).astype(BF16)
-    return grad_input, gin, gout
+        layer_scale,
+        dw_kernel,
+    )
+    return grad_input.reshape(tile_rows, tile_cols, channels), gin, gout
 
 
 def body(

time: 176 us -> 135 us (0.77)
  Pallas kernels: 139 us -> 128 us
  other arithmetic: 8.86 us -> 0 us
  waiting for transfers between devices: 8.08 us -> 0 us
  starting transfers between devices: 6.33 us -> 0 us
  local copies, waits for them, and re-layouts: 10.3 us -> 5.24 us
    pallas_call x1, Pallas kernels: 139 us -> 128 us  [fast_body(): pl.pallas_call(functools.partial(block_kernel, factor, tile_cols), out_sh...]
    ppermute x4 -> x0, waiting for transfers between devices: 8.08 us -> none  [the longest x2 7.25 us: with_halo(): lax.ppermute(lax.slice_in_dim(block, 0, width, axis=dim), axis, backward)]
    convert_element_type x2 -> x0, other arithmetic: 7.7 us -> none  [the longest x1 7.31 us: fast_body(): grad_input = (out_grad.astype(F32) + transpose_conv(padded.astype(F32), d...]
    ppermute x4 -> x0, starting transfers between devices: 6.33 us -> none  [the longest x2 3.75 us: with_halo(): lax.ppermute(lax.slice_in_dim(block, block.shape[dim] - width, None, axis...]
    reshape x4 -> x0, local copies, waits for them, and re-layouts: 5.15 us -> none  [the longest x1 1.29 us: fast_body(): layer_norm_gain.reshape(1, channels)]
    unnamed x10 -> x5, local copies, waits for them, and re-layouts: 2.71 us -> 5.24 us
    slice x4 -> x0, local copies, waits for them, and re-layouts: 2.46 us -> none  [the longest x3 1.41 us: transpose_conv(): dw_kernel[row_tap, col_tap]]
  transfers between devices with their start and end apart: 4 -> 0, of which waited for: 3 -> 0; matrix products, arithmetic and copies ran while one was open for 1% -> 0% of each run, Pallas kernels for 0% -> 0%
where the time goes in v2:
time: 135 us; the launch traced here: 134 us
  Pallas kernels  128 us (95%)
  local copies, waits for them, and re-layouts  5.24 us (4%)
    pallas_call x1, Pallas kernels, fast_body(): pl.pallas_call(functools.partial(block_kernel, factor, tile_cols), out_sh...  128 us
    unnamed x5, local copies, waits for them, and re-layouts  5.24 us

profile of v2, /device:TPU:0, one launch (start us, length us, event | category | flops | bytes accessed | tf_op | source)
XLA Modules:
  0.0 133.8 jit_solution(16385911970298174611)
XLA Ops:
  0.6 127.9 %shard_map.112 = (bf16[128,1536]{1,0:T(8,128)(2,1)}, f32[384,768]{1,0:T(8,128)}, f32[768,384]{1,0:T(8,128)}) custom-call(bf16[128,1536]{1,0:T(8,128)(2,1)} %bitcast.4, bf16[128,1536]{1,0:T(8,128)(2,1)} %bitcast.5, f32[1536]{0:T(1024)} %gain_ref.1, f32[1536]{0:T(1024)} %bias_ref.1, bf16[384,768]{1,0:T(8,128)(2,1)} %win_ref.1, f32[768]{0:T(1024)} %bin_ref.1, ...), custom_call_target="tpu_custom_call" | custom-call | flops 12079595520 | bytes 4718592 | tf_op jit(solution)/shard_map/pallas_call | solution.py:544
  128.5 1.8 %copy.15 = bf16[8,16,1536]{2,1,0:T(8,128)(2,1)} copy(bf16[8,16,1536]{2,1,0:T(8,128)(2,1)} %bitcast.3) | data formatting | bytes 786432
  130.3 0.0 copy-start
  130.3 2.5 %copy.16 = f32[384,768]{1,0:T(8,128)} copy(f32[384,768]{1,0:T(8,128)} %get-tuple-element.13) | data formatting | bytes 2359296
  132.8 0.0 copy-done
  132.8 1.0 copy.17
Async XLA Ops:
  130.3 2.5 %copy-start = (f32[768,384]{1,0:T(8,128)S(1)}, f32[768,384]{1,0:T(8,128)}, u32[]{:S(2)}) copy-start(f32[768,384]{1,0:T(8,128)} %get-tuple-element.14) | copy-start | bytes 3538948
